TPU v7x, 32 devices: a whole 2x2x4 slice. The times are simulated.
32 devices in a mesh: dp: 8 (over z, x), mp: 4 (over y, core).
Axes of the slice: x: 2, y: 2, z: 4, core: 2. Of those that a mesh axis runs over, the one named last changes fastest.
Arguments:
- tokens: bfloat16 [32768, 768], P(('dp', 'mp')), may hold values from -6 to 6
- segments: int32 [64, 512], P(('dp', 'mp')), may hold values from 0 to 5, never falling along the last dimension, each value on 1 to 256 neighbouring positions
- head_mask: int32 [12], replicated, may hold values 0 or 1
- unit_mask: int32 [3072], replicated, may hold values 0 or 1
- hidden_mask: int32 [768], replicated, may hold values 0 or 1
- layer_gates: float32 [2], replicated, may hold values from 0.5 to 1.5
- qkv_weight: bfloat16 [768, 2304], P('mp'), may hold values from -0.21875 to 0.21875
- out_weight: bfloat16 [768, 768], P('mp'), may hold values from -1.75 to 1.75
- norm_gain: float32 [768], replicated, may hold values from 0.5 to 1.5
- norm_bias: float32 [768], replicated, may hold values from -3 to 3
- up_weight: bfloat16 [768, 3072], P(None, 'mp'), may hold values from -0.21875 to 0.21875
- down_weight: bfloat16 [768, 3072], P(None, 'mp'), may hold values from -0.109375 to 0.109375
- cotangent: bfloat16 [32768, 768], P(('dp', 'mp')), may hold values from -6 to 6
- owner_slot: int32 [48], replicated, may hold values from 0 to 47, as said below
- master: float32 [48, 384, 384], P('dp', 'mp'), may hold values from -0.21875 to 0.21875
- left_stats: float32 [48, 384, 384], P('dp', 'mp'), may hold values from -12582912 to 50331648
- right_stats: float32 [48, 384, 384], P('dp', 'mp'), may hold values from -12582912 to 50331648
- left_root: float32 [48, 384, 384], P('dp', 'mp'), may hold values from -1 to 1
- right_root: float32 [48, 384, 384], P('dp'), may hold values from -1 to 1
Outputs:
- output: bfloat16 [32768, 768], P(('dp', 'mp'))
- input_grad: float32 [32768, 768], P(('dp', 'mp'))
- head_grad: float32 [12], replicated
- unit_grad: float32 [3072], replicated
- hidden_grad: float32 [768], replicated
- layer_grad: float32 [2], replicated
- norm_grad: float32 [2, 768], replicated
- norm_new: float32 [2, 768], replicated
- block_grad: float32 [48, 384, 384], P('dp', 'mp')
- left_new: float32 [48, 384, 384], P('dp', 'mp')
- right_new: float32 [48, 384, 384], P('dp', 'mp')
- weight_new: float32 [48, 384, 384], P('dp', 'mp')
- weight_copy: bfloat16 [48, 384, 384], P('dp', 'mp')
Inputs may be any that keep to these rules, and one draw needn't show every extreme that they name: `segments`: in every block of 512 positions the item numbers run from 0 to 5 and never fall; each item has 1 to 256 positions, and one item of each block has exactly 256. `owner_slot`: every slot number appears exactly once.
All inputs are finite; a program needn't handle non-finite values.
Results may differ from a plain program's by a relative error of at most 0.017.
Values may be sent and summed in bfloat16 or wider, within the bound.
A program may use at most 192 MiB of HBM per device.

v0:
```python
from functools import partial
import math
import jax
import jax.numpy as jnp
from jax import lax
from jax.sharding import PartitionSpec as P

FF = 3072
SB = 384
HIGH = lax.Precision.HIGHEST
BETA = 0.5
RATE = 0.5
EPS = 1e-12
MASKED = -1e30


def gelu_exact(values):
    return jax.nn.gelu(values, approximate=False)


def normalize(summed, gain_in, offset, hidden_gate):
    centre = summed - jnp.mean(summed, axis=-1, keepdims=True)
    spread = jnp.mean(centre * centre, axis=-1, keepdims=True)
    return (centre * lax.rsqrt(spread + EPS) * gain_in + offset) * hidden_gate


def split_heads(block_joined, head_count):
    pieces = block_joined.reshape(block_joined.shape[0], 3, head_count, -1)
    return (pieces[:, 0], pieces[:, 1], pieces[:, 2])


def masked_scores(queries, keys_in, labels, factor):
    scores = (
        jnp.einsum("qhd,khd->hqk", queries, keys_in, preferred_element_type=jnp.float32) * factor
    )
    allowed = labels[:, None] == labels[None, :]
    return jnp.where(allowed[None], scores, MASKED)


def attend_forward(packed, head_count, factor):
    block_joined, labels = packed
    queries, keys_in, values_in = split_heads(block_joined, head_count)
    scores = masked_scores(queries, keys_in, labels, factor)
    highest = jnp.max(scores, axis=-1, keepdims=True)
    raised = jnp.exp(scores - highest)
    totals = jnp.sum(raised, axis=-1, keepdims=True)
    weights_low = (raised / totals).astype(jnp.bfloat16)
    context = jnp.einsum("hqk,khd->qhd", weights_low, values_in, preferred_element_type=jnp.float32)
    return (context, (highest + jnp.log(totals))[:, :, 0])


def attend_backward(packed, head_count, factor):
    block_joined, log_totals, context_grad, labels = packed
    queries, keys_in, values_in = split_heads(block_joined, head_count)
    scores = masked_scores(queries, keys_in, labels, factor)
    weights_full = jnp.exp(scores - log_totals[:, :, None])
    weights_low = weights_full.astype(jnp.bfloat16)
    values_grad = jnp.einsum(
        "hqk,qhd->khd", weights_low, context_grad, preferred_element_type=jnp.float32
    )
    weights_grad = jnp.einsum(
        "qhd,khd->hqk", context_grad, values_in, preferred_element_type=jnp.float32
    )
    inner_sum = jnp.sum(weights_full * weights_grad, axis=-1, keepdims=True)
    scores_grad = (weights_full * (weights_grad - inner_sum)).astype(jnp.bfloat16)
    queries_grad = (
        jnp.einsum("hqk,khd->qhd", scores_grad, keys_in, preferred_element_type=jnp.float32)
        * factor
    )
    keys_grad = (
        jnp.einsum("hqk,qhd->khd", scores_grad, queries, preferred_element_type=jnp.float32)
        * factor
    )
    merged = jnp.concatenate([queries_grad, keys_grad, values_grad], axis=1)
    return merged.reshape(merged.shape[0], -1).astype(jnp.bfloat16)


def contract_rows(left, right):
    return lax.dot_general(
        left, right, (((0,), (0,)), ((), ())), preferred_element_type=jnp.float32
    )


def contract_cols(left, right):
    return lax.dot_general(
        left, right, (((1,), (1,)), ((), ())), preferred_element_type=jnp.float32
    )


def body(
    tokens,
    segments,
    head_mask,
    unit_mask,
    hidden_mask,
    layer_gates,
    qkv_weight,
    out_weight,
    norm_gain,
    norm_bias,
    up_weight,
    down_weight,
    cotangent,
    owner_slot,
    master,
    left_stats,
    right_stats,
    left_root,
    right_root,
):
    row_count = tokens.shape[0]
    width = tokens.shape[1]
    head_count = head_mask.shape[0]
    head_width = width // head_count
    block_rows = segments.shape[1]
    block_count = segments.shape[0]
    factor = 1.0 / math.sqrt(head_width)
    model_size = lax.axis_size("mp")
    share = FF // model_size
    part_rows = SB // model_size
    total_tokens = row_count * lax.axis_size("dp") * model_size
    head_gate = head_mask.astype(jnp.float32)
    unit_gate = unit_mask.astype(jnp.float32)
    hidden_gate = hidden_mask.astype(jnp.float32)
    inputs = tokens.astype(jnp.float32)
    back_full = cotangent.astype(jnp.float32)
    qkv_full, out_full, up_full, down_full = (
        lax.all_gather(qkv_weight, "mp", axis=0, tiled=True),
        lax.all_gather(out_weight, "mp", axis=0, tiled=True),
        lax.all_gather(up_weight, "mp", axis=1, tiled=True),
        lax.all_gather(down_weight, "mp", axis=1, tiled=True),
    )
    joined_qkv = jnp.dot(tokens, qkv_full, preferred_element_type=jnp.float32).astype(jnp.bfloat16)
    joined_blocks = joined_qkv.reshape(block_count, block_rows, 3 * width)
    context, log_totals = lax.map(
        partial(attend_forward, head_count=head_count, factor=factor), (joined_blocks, segments)
    )
    context = context.reshape(row_count, head_count, head_width)
    gated_low = (context * head_gate[None, :, None]).reshape(row_count, width).astype(jnp.bfloat16)
    attn_out = jnp.dot(gated_low, out_full, preferred_element_type=jnp.float32)
    summed = inputs + layer_gates[0] * attn_out
    hidden, norm_pull = jax.vjp(normalize, summed, norm_gain, norm_bias, hidden_gate)
    hidden_low = hidden.astype(jnp.bfloat16)
    pre_act = jnp.dot(hidden_low, up_full, preferred_element_type=jnp.float32)
    active, gelu_pull = jax.vjp(gelu_exact, pre_act)
    active_low = (active * unit_gate).astype(jnp.bfloat16)
    branch = contract_cols(active_low, down_full)
    output = (hidden + layer_gates[1] * branch).astype(jnp.bfloat16)
    back_rounded = (layer_gates[1] * back_full).astype(jnp.bfloat16)
    qkv_full, out_full, up_full, down_full = (
        lax.all_gather(qkv_weight, "mp", axis=0, tiled=True),
        lax.all_gather(out_weight, "mp", axis=0, tiled=True),
        lax.all_gather(up_weight, "mp", axis=1, tiled=True),
        lax.all_gather(down_weight, "mp", axis=1, tiled=True),
    )
    grad_active = jnp.dot(back_rounded, down_full, preferred_element_type=jnp.float32)
    unit_grad = jnp.sum(grad_active * active, axis=0)
    grad_inner = gelu_pull(grad_active * unit_gate)[0].astype(jnp.bfloat16)
    hidden_back = contract_cols(grad_inner, up_full)
    up_term = contract_rows(grad_inner, hidden_low)
    down_term = contract_rows(active_low, back_rounded)
    unit_local = (
        lax.psum_scatter(
            jnp.stack([up_term, down_term], axis=1).astype(jnp.bfloat16),
            "mp",
            scatter_dimension=0,
            tiled=True,
        )
        .astype(jnp.float32)
        .transpose(1, 2, 0)
    )
    summed_grad, gain_grad, bias_grad, mask_grad = norm_pull(back_full + hidden_back)
    layer_grad = jnp.stack([jnp.sum(summed_grad * attn_out), jnp.sum(back_full * branch)])
    out_back = (layer_gates[0] * summed_grad).astype(jnp.bfloat16)
    gated_grad = contract_cols(out_back, out_full).astype(jnp.bfloat16)
    gated_heads = gated_grad.reshape(row_count, head_count, head_width)
    head_grad = jnp.sum(context * gated_heads.astype(jnp.float32), axis=(0, 2))
    context_grad = gated_heads * head_mask.astype(jnp.bfloat16)[None, :, None]
    joined_grad = lax.map(
        partial(attend_backward, head_count=head_count, factor=factor),
        (
            joined_blocks,
            log_totals,
            context_grad.reshape(block_count, block_rows, head_count, head_width),
            segments,
        ),
    )
    joined_grad = joined_grad.reshape(row_count, 3 * width)
    input_grad = summed_grad + contract_cols(joined_grad, qkv_full)
    tiles = width // SB
    qkv_term = jnp.einsum(
        "tri,tcj->rcij",
        tokens.reshape(row_count, tiles, SB),
        joined_grad.reshape(row_count, 3 * tiles, SB),
        preferred_element_type=jnp.float32,
    )
    out_term = jnp.einsum(
        "tri,tcj->rcij",
        gated_low.reshape(row_count, tiles, SB),
        out_back.reshape(row_count, tiles, SB),
        preferred_element_type=jnp.float32,
    )
    attn_terms = jnp.concatenate(
        [
            qkv_term.reshape(-1, model_size, part_rows, SB),
            out_term.reshape(-1, model_size, part_rows, SB),
        ],
        axis=0,
    )
    attn_rows = (
        lax.psum_scatter(attn_terms.astype(jnp.bfloat16), "mp", scatter_dimension=1, tiled=True)
        .astype(jnp.float32)
        .reshape(-1, part_rows, SB)
    )
    unit_split = unit_local.reshape(2, tiles, model_size, part_rows, share)
    unit_rows = lax.all_to_all(
        unit_split.astype(jnp.bfloat16), "mp", split_axis=2, concat_axis=4, tiled=True
    ).astype(unit_split.dtype)
    unit_rows = (
        unit_rows.reshape(2, tiles, part_rows, FF // SB, SB)
        .transpose(0, 1, 3, 2, 4)
        .reshape(-1, part_rows, SB)
    )
    all_rows = jnp.concatenate([attn_rows, unit_rows], axis=0)
    slot_order = jnp.argsort(owner_slot)
    slotted = jnp.take(all_rows, slot_order, axis=0)
    owned = lax.psum_scatter(
        slotted.astype(jnp.bfloat16), "dp", scatter_dimension=0, tiled=True
    ).astype(jnp.float32)
    full_grad = lax.all_gather(owned.astype(jnp.bfloat16), "mp", axis=1, tiled=True).astype(
        owned.dtype
    )
    row_start = lax.axis_index("mp") * part_rows
    columns = lax.dynamic_slice_in_dim(full_grad, row_start, part_rows, 2)
    left_new = BETA * left_stats + (1.0 - BETA) * jnp.einsum(
        "srj,skj->srk", owned, full_grad, precision=HIGH
    )
    right_new = BETA * right_stats + (1.0 - BETA) * jnp.einsum(
        "sjr,sjk->srk", columns, full_grad, precision=HIGH
    )
    left_part = jnp.einsum("sri,sij->srj", left_root, full_grad, precision=HIGH)
    update = jnp.einsum("srj,sjk->srk", left_part, right_root, precision=HIGH)
    weight_new = master - RATE * update
    norm_grad = jnp.stack([gain_grad, bias_grad])
    norm_grad, mask_grad, head_grad, layer_grad, unit_grad = lax.psum(
        (norm_grad, mask_grad, head_grad, layer_grad, unit_grad), ("dp", "mp")
    )
    norm_new = jnp.stack([norm_gain, norm_bias]) - 0.2 / math.sqrt(total_tokens) * norm_grad
    return (
        output,
        input_grad,
        head_grad,
        unit_grad,
        mask_grad,
        layer_grad,
        norm_grad,
        norm_new,
        owned,
        left_new,
        right_new,
        weight_new,
        weight_new.astype(jnp.bfloat16),
    )


def solution(mesh):
    return jax.shard_map(
        body,
        mesh=mesh,
        in_specs=(
            P(("dp", "mp"), None),
            P(("dp", "mp"), None),
            P(),
            P(),
            P(),
            P(),
            P("mp", None),
            P("mp", None),
            P(),
            P(),
            P(None, "mp"),
            P(None, "mp"),
            P(("dp", "mp"), None),
            P(),
            P("dp", "mp", None),
            P("dp", "mp", None),
            P("dp", "mp", None),
            P("dp", "mp", None),
            P("dp", None, None),
        ),
        out_specs=(
            P(("dp", "mp"), None),
            P(("dp", "mp"), None),
            P(),
            P(),
            P(),
            P(),
            P(),
            P(),
            P("dp", "mp", None),
            P("dp", "mp", None),
            P("dp", "mp", None),
            P("dp", "mp", None),
            P("dp", "mp", None),
        ),
        check_vma=False,
    )
```

profile of v0, /device:TPU:0, one launch (start us, length us, event | category | flops | bytes accessed | tf_op | source)
XLA Modules:
  0.0 672.5 jit_solution(17716247387969877652)
XLA Ops:
  12.6 2.6 copy.83
  16.4 2.6 copy.87
  19.6 23.5 %all-gather.6.cloned.1.call-done = bf16[768,2304]{1,0:T(8,128)(2,1)} async-done(((bf16[192,2304]{1,0:T(8,128)(2,1)}), bf16[768,2304]{1,0:T(8,128)(2,1)}) %all-gather.6.cloned.1.call-update) | async-done | bytes 3538960 | tf_op jit(solution)/shard_map/all_gather | solution.py:128
  43.1 8.4 %convolution_convert_fusion = bf16[1024,2304]{1,0:T(8,128)(2,1)} fusion(bf16[1024,768]{1,0:T(8,128)(2,1)} %param.23, bf16[768,2304]{1,0:T(8,128)(2,1)} %all-gather.6.cloned.1.call-done), kind=kOutput, calls=%fused_computation.70 | convolution fusion | flops 3626237952 | bytes 9830400 | tf_op jit(solution)/shard_map/dot_general | solution.py:133
  51.5 6.9 %copy.84 = bf16[2,512,2304]{1,2,0:T(8,128)(2,1)} copy(bf16[2,512,2304]{2,1,0:T(8,128)(2,1)} %bitcast.203) | data formatting | bytes 9437184 | tf_op jit(solution)/shard_map/while | solution.py:135
  58.4 28.8 %while.22 = (s32[]{:T(128)}, f32[2,512,12,64]{1,3,2,0:T(8,128)}, f32[2,12,512]{2,1,0:T(8,128)}, bf16[2,512,2304]{1,2,0:T(8,128)(2,1)}, s32[2,512]{1,0:T(2,128)S(1)}, /*index=5*/s32[]{:T(128)}) while((s32[]{:T(128)}, f32[2,512,12,64]{1,3,2,0:T(8,128)}, f32[2,12,512]{2,1,0:T(8,128)}, bf16[2,512,2304]{1,2,0:T(8,128)(2,1)}, ...), condition=%wide.region_3.4_spmd, body=%wide.region_0.3_spmd.sunk | while | flops 843311104 | bytes 58145924 | solution.py:135
  60.6 2.1 fusion.100
  62.7 3.5 fusion.101
  66.9 5.6 bitcast_dynamic-update-slice_fusion.4
  72.7 2.1 constant_dynamic-slice_fusion.9
  74.9 2.1 fusion.100
  77.0 3.5 fusion.101
  81.2 5.6 bitcast_dynamic-update-slice_fusion.4
  87.2 4.4 copy.85
  91.6 2.4 copy.125
  94.6 2.7 copy.99
  97.3 3.8 reshape.267
  101.1 6.7 %fusion.57 = (f32[1024]{0:T(1024)S(1)}, f32[1024,768]{0,1:T(8,128)S(1)}, f32[1024,768]{0,1:T(8,128)}) fusion(f32[]{:T(128)} %bitcast.19, bf16[1024,768]{0,1:T(8,128)(2,1)} %copy.83, bf16[768,768]{1,0:T(8,128)(2,1)} %all-gather.8.cloned.1.call-done, f32[1024,768]{0,1:T(8,128)} %bitcast.196, f32[768]{0:T(1024)S(1)} %mul.224), kind=kOutput, calls=%fused_computation.130 | convolution fusion | flops 1212677120 | bytes 12196868 | tf_op jit(solution)/shard_map/dot_general | solution.py:140
  110.5 12.1 %fusion.54 = f32[1024,3072]{1,0:T(8,128)} fusion(bf16[768,3072]{1,0:T(8,128)(2,1)} %all-gather.10.cloned.1.call-done, f32[1024,768]{0,1:T(8,128)} %copy-done.5, f32[768]{0:T(1024)S(1)} %copy-done.30, f32[768]{0:T(1024)} %param.32, f32[768]{0:T(1024)S(1)} %copy-done.27, f32[1024]{0:T(1024)S(1)} %fusion.52, f32[1024]{0:T(1024)S(1)} %broadcast_multiply_fusion.1), kind=kOutput, calls=%fused_computation.128 | convolution fusion | flops 4836556800 | bytes 20464640 | tf_op jit(solution)/shard_map/dot_general | solution.py:144
  122.6 17.5 %all-gather.12.cloned.1.call-done = bf16[768,3072]{1,0:T(8,128)(2,1)} async-done(((bf16[768,768]{1,0:T(8,128)(2,1)}), bf16[768,3072]{1,0:T(8,128)(2,1)}) %all-gather.12.cloned.1.call-update) | async-done | bytes 4718608 | tf_op jit(solution)/shard_map/all_gather | solution.py:131
  140.1 38.9 %multiply_reduce_fusion.1 = (f32[3072]{0:T(1024)}, f32[1024,3072]{1,0:T(8,128)}, f32[1024,3072]{1,0:T(8,128)}) fusion(f32[1024,3072]{1,0:T(8,128)} %fusion.54, bf16[768,3072]{1,0:T(8,128)(2,1)} %all-gather.12.cloned.1.call-done, bf16[1024,768]{0,1:T(8,128)(2,1)} %copy.87, f32[]{:T(128)} %bitcast.21), kind=kOutput, calls=%fused_computation.51 | convolution fusion | flops 5041812480 | bytes 44052484 | tf_op jit(solution)/shard_map/dot_general | solution.py:156
  179.1 16.6 %add_convert_fusion = (bf16[1024,3072]{1,0:T(8,128)(2,1)}, bf16[1024,3072]{1,0:T(8,128)(2,1)}) fusion(f32[1024,3072]{1,0:T(8,128)} %get-tuple-element.182, f32[1024,3072]{1,0:T(8,128)} %get-tuple-element.202, f32[1024,3072]{1,0:T(8,128)S(1)} %bitcast.193, f32[3072]{0:T(1024)S(1)} %copy-done.40), kind=kLoop, calls=%fused_computation.52 | loop fusion | flops 56623104 | bytes 50343936 | tf_op jit(solution)/shard_map/convert_element_type | solution.py:158
  195.8 10.6 %fusion.36 = bf16[3072,1,768]{2,0,1:T(8,128)(2,1)} fusion(bf16[1024,3072]{1,0:T(8,128)(2,1)} %get-tuple-element.191, f32[1024,768]{0,1:T(8,128)S(1)} %copy-done.6, f32[768]{0:T(1024)S(1)} %copy-done.31, f32[768]{0:T(1024)S(1)} %copy-done.35, f32[768]{0:T(1024)S(1)} %copy-done.28, f32[1024]{0:T(1024)S(1)} %copy-done.33, f32[1024]{0:T(1024)S(1)} %copy-done.26), kind=kOutput, calls=%fused_computation.80 | convolution fusion | flops 4838916096 | bytes 14173184 | tf_op jit(solution)/shard_map/dot_general | solution.py:79
  206.4 7.7 %fusion.37 = bf16[3072,1,768]{2,0,1:T(8,128)(2,1)} fusion(bf16[1024,3072]{1,0:T(8,128)(2,1)S(1)} %copy-done.13, bf16[1024,768]{0,1:T(8,128)(2,1)S(1)} %copy-done.17, f32[]{:T(128)} %bitcast.21), kind=kOutput, calls=%fused_computation.81 | convolution fusion | flops 4836556800 | bytes 12582916 | tf_op jit(solution)/shard_map/dot_general | solution.py:79
  214.1 8.2 %pad_maximum_fusion.1 = bf16[3072,2,768]{2,0,1:T(8,128)(2,1)} fusion(bf16[3072,1,768]{2,0,1:T(8,128)(2,1)} %fusion.37, bf16[3072,1,768]{2,0,1:T(8,128)(2,1)} %fusion.36), kind=kLoop, calls=%fused_computation.68 | loop fusion | flops 4718592 | bytes 18874368 | tf_op jit(solution)/shard_map/stack | solution.py:164
  222.5 8.7 %fusion.61 = f32[1024,768]{0,1:T(8,128)S(1)} fusion(bf16[1024,3072]{1,0:T(8,128)(2,1)} %get-tuple-element.192, bf16[768,3072]{1,0:T(8,128)(2,1)} %all-gather.12.cloned.1.call-done), kind=kOutput, calls=%fused_computation.134 | convolution fusion | flops 4831838208 | bytes 14155776 | tf_op jit(solution)/shard_map/dot_general | solution.py:85
  231.2 14.8 %multiply_reduce_fusion.2 = (f32[768]{0:T(1024)}, f32[1024]{0:T(1024)S(1)}, f32[768]{0:T(1024)}, f32[768]{0:T(1024)}, bf16[1024,768]{0,1:T(8,128)(2,1)}, /*index=5*/f32[]{:T(128)}, f32[1024,768]{0,1:T(8,128)S(1)}) fusion(f32[1024,768]{0,1:T(8,128)S(1)} %copy-done.7, f32[768]{0:T(1024)S(1)} %copy-done.31, f32[1024]{0:T(1024)S(1)} %copy-done.33, ...), kind=kOutput, calls=%fused_computation.87 | convolution fusion | flops 4848349184 | bytes 23623688 | tf_op jit(solution)/shard_map/dot_general | solution.py:85
  247.0 2.6 copy-done.12
  249.5 2.4 multiply_reduce_fusion.3
  253.1 2.6 convolution_convert_fusion.3
  255.7 2.6 copy.88
  258.4 3.9 reshape.245
  262.2 3.0 broadcast_multiply_fusion
  266.7 55.7 %while.23 = (s32[]{:T(128)}, bf16[2,512,2304]{1,2,0:T(8,128)(2,1)}, bf16[2,512,2304]{1,2,0:T(8,128)(2,1)}, s32[2,512]{1,0:T(2,128)S(1)}, f32[2,12,512]{2,1,0:T(8...) while((s32[]{:T(128)}, bf16[2,512,2304]{1,2,0:T(8,128)(2,1)}, bf16[2,512,2304]{1,2,0:T(8,128)(2,1)}, ...), condition=%wide.region_10.11_spmd, body=%wide.region_8.10_spmd.sunk | while | flops 2065033216 | bytes 142990544 | solution.py:179
  271.3 7.0 %multiply_reduce_fusion.10 = (f32[12,512]{1,0:T(8,128)S(1)}, f32[12,512,512]{1,2,0:T(8,128)}) fusion(f32[12,512,512]{1,2,0:T(8,128)S(1)} %fusion.106, f32[12,512]{1,0:T(8,128)S(1)} %dynamic-slice_bitcast_fusion.3, pred[512,512]{0,1:T(8,128)(4,1)S(1)} %broadcast_compare_fusion.5, bf16[512,3,12,64]{0,3,2,1:T(8,128)(2,1)S(1)} %bitcast.186, ...), kind=kOutput, calls=%fused_computation.19.clone.1 | convolution fusion | flops 418375680 | bytes 27058180 | tf_op jit(solution)/shard_map/while/body/eval_jaxpr/qhd,khd->hqk/dot_general | solution.py:61
  278.3 7.1 %multiply_convert_fusion.12 = bf16[12,512,512]{1,2,0:T(8,128)(2,1)S(1)} fusion(f32[12,512,512]{1,2,0:T(8,128)} %get-tuple-element.280, f32[12,512,512]{1,2,0:T(8,128)S(1)} %fusion.106, f32[12,512]{1,0:T(8,128)S(1)} %get-tuple-element.281, f32[12,512]{1,0:T(8,128)S(1)} %dynamic-slice_bitcast_fusion.3, pred[512,512]{0,1:T(8,128)(4,1)S(1)} %broadcast_compare_fusion.5), kind=kLoop, calls=%fused_computation.18.clone.1 | loop fusion | flops 18874368 | bytes 31768576 | tf_op jit(solution)/shard_map/while/body/eval_jaxpr/convert_element_type | solution.py:65
  288.6 4.3 fusion.107
  298.9 7.0 %multiply_reduce_fusion.10 = (f32[12,512]{1,0:T(8,128)S(1)}, f32[12,512,512]{1,2,0:T(8,128)}) fusion(f32[12,512,512]{1,2,0:T(8,128)S(1)} %fusion.106, f32[12,512]{1,0:T(8,128)S(1)} %dynamic-slice_bitcast_fusion.3, pred[512,512]{0,1:T(8,128)(4,1)S(1)} %broadcast_compare_fusion.5, bf16[512,3,12,64]{0,3,2,1:T(8,128)(2,1)S(1)} %bitcast.186, ...), kind=kOutput, calls=%fused_computation.19.clone.1 | convolution fusion | flops 418375680 | bytes 27058180 | tf_op jit(solution)/shard_map/while/body/eval_jaxpr/qhd,khd->hqk/dot_general | solution.py:61
  305.9 7.1 %multiply_convert_fusion.12 = bf16[12,512,512]{1,2,0:T(8,128)(2,1)S(1)} fusion(f32[12,512,512]{1,2,0:T(8,128)} %get-tuple-element.280, f32[12,512,512]{1,2,0:T(8,128)S(1)} %fusion.106, f32[12,512]{1,0:T(8,128)S(1)} %get-tuple-element.281, f32[12,512]{1,0:T(8,128)S(1)} %dynamic-slice_bitcast_fusion.3, pred[512,512]{0,1:T(8,128)(4,1)S(1)} %broadcast_compare_fusion.5), kind=kLoop, calls=%fused_computation.18.clone.1 | loop fusion | flops 18874368 | bytes 31768576 | tf_op jit(solution)/shard_map/while/body/eval_jaxpr/convert_element_type | solution.py:65
  316.2 4.3 fusion.107
  322.4 9.9 %copy.95 = bf16[2,512,2304]{1,0,2:T(2,128)(2,1)} copy(bf16[2,512,2304]{1,2,0:T(8,128)(2,1)} %get-tuple-element.76) | data formatting | bytes 9437184 | tf_op jit(solution)/shard_map/while | solution.py:179
  332.3 8.7 %reshape_reshape.3 = bf16[1024,6,384]{0,2,1:T(8,128)(2,1)} reshape(bf16[2,512,2304]{1,0,2:T(2,128)(2,1)} %copy.95) | data formatting | bytes 9437184 | tf_op jit(solution)/shard_map/reshape;reshape | solution.py:194
  341.0 6.8 %convert_bitcast_fusion = bf16[2,6,384,384]{3,2,0,1:T(8,128)(2,1)S(1)} fusion(bf16[1024,2,384,1]{0,2,1,3:T(8,128)(2,1)} %bitcast.200, bf16[1024,6,384]{0,2,1:T(8,128)(2,1)} %reshape_reshape.3), kind=kOutput, calls=%fused_computation.83 | convolution fusion | flops 3625648128 | bytes 9830400 | tf_op jit(solution)/shard_map/tri,tcj->rcij/dot_general | solution.py:191
  351.2 2.7 pad_maximum_fusion.2
  354.0 4.3 copy.102
  358.3 3.9 copy.103
  362.2 4.6 all-to-all-start
  369.6 103.6 %all-reduce.4.cloned.1.call-done = bf16[16,4,96,384]{3,2,1,0:T(8,128)(2,1)} async-done(((bf16[16,4,96,384]{3,2,1,0:T(8,128)(2,1)}), bf16[16,4,96,384]{3,2,1,0:T(8,128)(2,1)}) %all-reduce.4.cloned.1.call-update) | async-done | bytes 4718608
  473.2 3.1 dynamic-slice_bitcast_fusion.1
  476.2 4.9 copy.104
  481.1 5.2 convert_element_type.132
  486.3 2.1 copy.105
  488.4 2.2 maximum_convert_fusion
  490.6 5.1 gather_fusion
  495.6 4.9 select_convert_fusion
  500.7 79.4 %reduce-scatter.8.cloned.1.call-done = bf16[6,96,384]{2,1,0:T(8,128)(2,1)} async-done(((bf16[48,96,384]{2,1,0:T(8,128)(2,1)}), bf16[6,96,384]{2,1,0:T(8,128)(2,1)}) %reduce-scatter.8.cloned.1.call-update) | async-done | bytes 442384 | tf_op jit(solution)/shard_map/reduce_scatter | solution.py:227
  583.4 5.5 multiply_reduce_fusion.5
  588.9 41.4 %all-reduce.1 = (f32[12]{0:T(128)}, f32[3072]{0:T(1024)}, f32[768]{0:T(1024)}, f32[2]{0:T(128)}, f32[2,768]{1,0:T(2,128)}) all-reduce(f32[12]{0:T(128)} %multiply_reduce_fusion.5, f32[3072]{0:T(1024)} %get-tuple-element.181, f32[768]{0:T(1024)} %get-tuple-element.152, ...), channel_id=1, replica_groups=mesh['dp'=8,'mp'=4] {'dp','mp'}, use_global_device_ids=true, to_apply=%region_12.13 | all-reduce | flops 5390 | bytes 43120 | tf_op jit(solution)/shard_map/psum | solution.py:245
  630.3 6.7 copy.91
  637.0 9.8 %add_add_fusion.1 = f32[1024,768]{0,1:T(8,128)} fusion(f32[1024,768]{0,1:T(8,128)} %copy-done.11, bf16[1024,2304]{1,0:T(8,128)(2,1)} %bitcast.202, bf16[768,2304]{1,0:T(8,128)(2,1)} %all-gather.6.cloned.1.call-done, f32[1024]{0:T(1024)S(1)} %copy-done.44), kind=kOutput, calls=%fused_computation.99 | convolution fusion | flops 3625451520 | bytes 14553088 | tf_op jit(solution)/shard_map/dot_general | solution.py:85
  646.8 3.6 copy.108
  650.4 2.6 copy.107
  655.5 2.9 fusion.62
  658.5 3.6 fusion.60
  (206 shorter events, 51.3 us)
Async XLA Ops:
  7.2 651.3 %copy-start = (f32[6,384,384]{2,1,0:T(8,128)S(1)}, f32[6,384,384]{2,1,0:T(8,128)}, u32[]{:S(2)}) copy-start(f32[6,384,384]{2,1,0:T(8,128)} %param.41) | copy-start | bytes 10616836
  7.2 2.9 copy-start.50
  7.2 35.9 %all-gather.6.cloned.1.call-start = ((), (), s32[]{:S(2)}) async-start(), calls=%async_computation.3 | async-start | bytes 4423680 | tf_op jit(solution)/shard_map/all_gather | solution.py:128
  7.9 93.2 %all-gather.8.cloned.1.call-start = ((), (), s32[]{:S(2)}) async-start(), calls=%async_computation.4 | async-start | bytes 1474560 | tf_op jit(solution)/shard_map/all_gather | solution.py:129
  8.7 101.8 %all-gather.10.cloned.1.call-start = ((), (), s32[]{:S(2)}) async-start(), calls=%async_computation.5 | async-start | bytes 5898240 | tf_op jit(solution)/shard_map/all_gather | solution.py:130
  9.4 130.7 %all-gather.12.cloned.1.call-start = ((), (), s32[]{:S(2)}) async-start(), calls=%async_computation.6 | async-start | bytes 5898240 | tf_op jit(solution)/shard_map/all_gather | solution.py:131
  10.0 344.0 %reduce-scatter.6.cloned.1.call-start = ((), (), s32[]{:S(2)}) async-start(), calls=%async_computation.7 | async-start | bytes 11796480 | tf_op jit(solution)/shard_map/reduce_scatter | solution.py:163
  11.3 7.8 %copy-start.45 = (s32[3072]{0:T(1024)S(1)}, s32[3072]{0:T(1024)}, u32[]{:S(2)}) copy-start(s32[3072]{0:T(1024)} %param.26) | copy-start | bytes 36868
  51.5 6.9 %copy-start.38 = (s32[2,512]{1,0:T(2,128)S(1)}, s32[2,512]{1,0:T(2,128)}, u32[]{:S(2)}) copy-start(s32[2,512]{1,0:T(2,128)} %param.24) | copy-start | bytes 12292
  58.6 4.1 copy-start.4
  60.6 2.1 copy-start.3
  72.7 4.3 copy-start.4
  74.8 2.1 copy-start.3
  91.6 2.4 copy-start.8
  91.6 2.4 copy-start.48
  101.1 9.4 %copy-start.27 = (f32[768]{0:T(1024)S(1)}, f32[768]{0:T(1024)}, u32[]{:S(2)}) copy-start(f32[768]{0:T(1024)} %param.31) | copy-start | bytes 9220
  101.1 9.4 %copy-start.30 = (f32[768]{0:T(1024)S(1)}, f32[768]{0:T(1024)}, u32[]{:S(2)}) copy-start(f32[768]{0:T(1024)} %convert_element_type.114) | copy-start | bytes 9220
  107.9 14.7 %copy-start.25 = (f32[1024]{0:T(1024)}, f32[1024]{0:T(1024)S(1)}, u32[]{:S(2)}) copy-start(f32[1024]{0:T(1024)S(1)} %broadcast_multiply_fusion.1) | copy-start | bytes 12292
  110.4 12.1 %copy-start.32 = (f32[1024]{0:T(1024)}, f32[1024]{0:T(1024)S(1)}, u32[]{:S(2)}) copy-start(f32[1024]{0:T(1024)S(1)} %fusion.52) | copy-start | bytes 12292
  140.1 38.9 %slice-start = ((s8[12582912]{0:T(1024)(128)(4,1)}), s8[4194304]{0:T(1024)(128)(4,1)S(1)}, s32[]{:S(2)}) async-start(s8[12582912]{0:T(1024)(128)(4,1)} %bitcast.192), calls=%async_computation.11 | async-start | bytes 8388608
  140.1 38.9 %slice-start.1 = ((s8[12582912]{0:T(1024)(128)(4,1)}), s8[4194304]{0:T(1024)(128)(4,1)S(1)}, s32[]{:S(2)}) async-start(s8[12582912]{0:T(1024)(128)(4,1)} %bitcast.192), calls=%async_computation.12 | async-start | bytes 8388608
  140.1 38.9 %slice-start.2 = ((s8[12582912]{0:T(1024)(128)(4,1)}), s8[4194304]{0:T(1024)(128)(4,1)S(1)}, s32[]{:S(2)}) async-start(s8[12582912]{0:T(1024)(128)(4,1)} %bitcast.192), calls=%async_computation.13 | async-start | bytes 8388608
  140.1 38.9 %copy-start.40 = (f32[3072]{0:T(1024)S(1)}, f32[3072]{0:T(1024)}, u32[]{:S(2)}) copy-start(f32[3072]{0:T(1024)} %convert_element_type.116) | copy-start | bytes 36868
  179.1 16.7 %copy-start.6 = (f32[1024,768]{0,1:T(8,128)S(1)}, f32[1024,768]{0,1:T(8,128)}, u32[]{:S(2)}) copy-start(f32[1024,768]{0,1:T(8,128)} %copy-done.5) | copy-start | bytes 9437188
  179.1 16.7 %copy-start.26 = (f32[1024]{0:T(1024)S(1)}, f32[1024]{0:T(1024)}, u32[]{:S(2)}) copy-start(f32[1024]{0:T(1024)} %copy-done.25) | copy-start | bytes 12292
  179.1 16.6 %copy-start.28 = (f32[768]{0:T(1024)S(1)}, f32[768]{0:T(1024)}, u32[]{:S(2)}) copy-start(f32[768]{0:T(1024)} %param.31) | copy-start | bytes 9220
  179.1 16.6 %copy-start.31 = (f32[768]{0:T(1024)S(1)}, f32[768]{0:T(1024)}, u32[]{:S(2)}) copy-start(f32[768]{0:T(1024)} %convert_element_type.114) | copy-start | bytes 9220
  179.1 16.6 %copy-start.33 = (f32[1024]{0:T(1024)S(1)}, f32[1024]{0:T(1024)}, u32[]{:S(2)}) copy-start(f32[1024]{0:T(1024)} %copy-done.32) | copy-start | bytes 12292
  179.1 16.6 %copy-start.35 = (f32[768]{0:T(1024)S(1)}, f32[768]{0:T(1024)}, u32[]{:S(2)}) copy-start(f32[768]{0:T(1024)} %param.32) | copy-start | bytes 9220
  195.8 10.6 %copy-start.13 = (bf16[1024,3072]{1,0:T(8,128)(2,1)S(1)}, bf16[1024,3072]{1,0:T(8,128)(2,1)}, u32[]{:S(2)}) copy-start(bf16[1024,3072]{1,0:T(8,128)(2,1)} %get-tuple-element.192) | copy-start | bytes 18874372
  195.8 10.6 %copy-start.17 = (bf16[1024,768]{0,1:T(8,128)(2,1)S(1)}, bf16[1024,768]{0,1:T(8,128)(2,1)}, u32[]{:S(2)}) copy-start(bf16[1024,768]{0,1:T(8,128)(2,1)} %copy.87) | copy-start | bytes 4718596
  222.4 250.8 %all-reduce.4.cloned.1.call-start = ((), (), s32[]{:S(2)}) async-start(), calls=%async_computation.10 | async-start | bytes 9437184
  222.4 8.8 %copy-start.7 = (f32[1024,768]{0,1:T(8,128)S(1)}, f32[1024,768]{0,1:T(8,128)}, u32[]{:S(2)}) copy-start(f32[1024,768]{0,1:T(8,128)} %copy-done.5) | copy-start | bytes 9437188
  222.4 8.8 %copy-start.18 = (bf16[1024,768]{0,1:T(8,128)(2,1)S(1)}, bf16[1024,768]{0,1:T(8,128)(2,1)}, u32[]{:S(2)}) copy-start(bf16[1024,768]{0,1:T(8,128)(2,1)} %copy.87) | copy-start | bytes 4718596
  222.4 8.8 %copy-start.36 = (f32[768]{0:T(1024)S(1)}, f32[768]{0:T(1024)}, u32[]{:S(2)}) copy-start(f32[768]{0:T(1024)} %param.32) | copy-start | bytes 9220
  231.2 14.8 %copy-start.42 = (f32[1024]{0:T(1024)S(1)}, f32[1024]{0:T(1024)}, u32[]{:S(2)}) copy-start(f32[1024]{0:T(1024)} %copy-done.41) | copy-start | bytes 12292
  246.0 3.5 copy-start.12
  246.9 5.0 copy-start.11
  247.0 5.0 copy-start.43
  249.5 3.5 copy-start.21
  255.7 6.5 copy-start.49
  262.2 4.5 copy-start.39
  268.9 2.1 copy-start.1
  268.9 2.1 copy-start.34
  269.0 2.4 copy-start.9
  278.3 7.1 %copy-start.2 = (bf16[1,512,2304]{1,2,0:T(8,128)(2,1)S(1)}, bf16[1,512,2304]{1,2,0:T(8,128)(2,1)}, u32[]{:S(2)}) copy-start(bf16[1,512,2304]{1,2,0:T(8,128)(2,1)} %copy-done.1) | copy-start | bytes 7077892 | tf_op jit(solution)/shard_map/while
  296.6 2.1 copy-start.1
  296.6 2.1 copy-start.34
  296.6 2.3 copy-start.9
  305.9 7.1 %copy-start.2 = (bf16[1,512,2304]{1,2,0:T(8,128)(2,1)S(1)}, bf16[1,512,2304]{1,2,0:T(8,128)(2,1)}, u32[]{:S(2)}) copy-start(bf16[1,512,2304]{1,2,0:T(8,128)(2,1)} %copy-done.1) | copy-start | bytes 7077892 | tf_op jit(solution)/shard_map/while
  362.2 4.7 copy-start.52
  362.2 5.3 copy-start.51
  362.2 114.0 %all-to-all-start = ((bf16[2,2,4,96,768]{4,3,1,0,2:T(8,128)(2,1)}), bf16[2,2,4,96,768]{4,3,1,0,2:T(8,128)(2,1)}, u32[]{:S(2)}, u32[]{:S(2)}) async-start(bf16[2,2,4,96,768]{4,3,1,0,2:T(8,128)(2,1)} %copy.103), calls=%async_computation.1 | async-start | bytes 4718592 | tf_op jit(solution)/shard_map/all_to_all | solution.py:216
  366.9 213.2 %reduce-scatter.8.cloned.1.call-start = ((), (), s32[]{:S(2)}) async-start(), calls=%async_computation.8 | async-start | bytes 3981312 | tf_op jit(solution)/shard_map/reduce_scatter | solution.py:227
  486.3 2.1 copy-start.14
  500.6 79.5 %copy-start.29 = (f32[768]{0:T(1024)S(1)}, f32[768]{0:T(1024)}, u32[]{:S(2)}) copy-start(f32[768]{0:T(1024)} %param.31) | copy-start | bytes 9220
  500.6 79.5 %copy-start.37 = (f32[768]{0:T(1024)S(1)}, f32[768]{0:T(1024)}, u32[]{:S(2)}) copy-start(f32[768]{0:T(1024)} %param.32) | copy-start | bytes 9220
  500.6 154.9 %all-gather.14.cloned.1.call-start = ((), (), s32[]{:S(2)}) async-start(), calls=%async_computation.9 | async-start | bytes 2211840 | tf_op jit(solution)/shard_map/all_gather | solution.py:230
  630.3 6.7 copy-start.44
  646.8 6.1 copy-start.46
  655.5 2.9 copy-start.22
  658.5 3.6 copy-start.10
  658.5 3.6 copy-start.15
  658.5 3.6 copy-start.23
  (7 other events, 8.8 us)
Sparse Core Ops, SparseCore 0:
  9.6 33.4 all-gather.5
  44.7 17.4 all-gather.7
  63.7 37.4 all-gather.9
  102.6 37.4 all-gather.11
  222.5 78.3 reduce-scatter.5
  354.1 119.0 all-reduce.3
  500.7 79.2 reduce-scatter.7
  581.6 20.8 all-gather.13
where the time goes:
time: 682 us; the launch traced here: 672 us
  waiting for transfers between devices  227 us (33%)
  matrix products  187 us (27%)
  local copies, waits for them, and re-layouts  117 us (17%)
  other arithmetic  80.2 us (12%)
  blocking collectives  41.4 us (6%)
  between operations  15 us (2%)
    unnamed x9, waiting for transfers between devices  106 us
    reduce_scatter x1, waiting for transfers between devices, body(): lax.psum_scatter(slotted.astype(jnp.bfloat16), 'dp', scatter_dimension=0,...  79.4 us
    psum x1, blocking collectives, body(): lax.psum((norm_grad, mask_grad, head_grad, layer_grad, unit_grad), ('dp',...  41.4 us
    dot_general x1, matrix products, body(): jnp.dot(back_rounded, down_full, preferred_element_type=jnp.float32)  38.9 us
    dot_general x4, matrix products, contract_cols(): lax.dot_general(left, right, (((1,), (1,)), ((), ())), preferred_element_...  35.9 us
    all_gather x1, waiting for transfers between devices, body(): lax.all_gather(qkv_weight, 'mp', axis=0, tiled=True)  23.5 us
    unnamed x106, local copies, waits for them, and re-layouts  22.4 us
    dot_general x2, matrix products, contract_rows(): lax.dot_general(left, right, (((0,), (0,)), ((), ())), preferred_element_...  18.3 us
  transfers between devices with their start and end apart: 9, of which 4 were waited for; matrix products, arithmetic and copies ran while one was open for 38% of the time, Pallas kernels for 0%

commit v1 on v0

--- a/solution.py
+++ b/solution.py
@@ -12,6 +12,27 @@
 RATE = 0.5
 EPS = 1e-12
 MASKED = -1e30
+
+
+def ring_gather(array, axis, dim):
+    size, index, rows = (lax.axis_size(axis), lax.axis_index(axis), array.shape[dim])
+    right = [(i, (i + 1) % size) for i in range(size)]
+    backward = [(i, (i - 1) % size) for i in range(size)]
+    filled = jnp.zeros((*array.shape[:dim], size * rows, *array.shape[dim + 1 :]), array.dtype)
+    filled = lax.dynamic_update_slice_in_dim(filled, array, index * rows, axis=dim)
+    from_left = from_right = array
+    halfway = size // 2
+    for turn in range(1, halfway + 1):
+        from_left = lax.ppermute(from_left, axis, right)
+        filled = lax.dynamic_update_slice_in_dim(
+            filled, from_left, (index - turn) % size * rows, axis=dim
+        )
+        if turn < size - halfway:
+            from_right = lax.ppermute(from_right, axis, backward)
+            filled = lax.dynamic_update_slice_in_dim(
+                filled, from_right, (index + turn) % size * rows, axis=dim
+            )
+    return filled
 
 
 def gelu_exact(values):
@@ -128,7 +149,7 @@
         lax.all_gather(qkv_weight, "mp", axis=0, tiled=True),
         lax.all_gather(out_weight, "mp", axis=0, tiled=True),
         lax.all_gather(up_weight, "mp", axis=1, tiled=True),
-        lax.all_gather(down_weight, "mp", axis=1, tiled=True),
+        ring_gather(down_weight, "mp", 1),
     )
     joined_qkv = jnp.dot(tokens, qkv_full, preferred_element_type=jnp.float32).astype(jnp.bfloat16)
     joined_blocks = joined_qkv.reshape(block_count, block_rows, 3 * width)

time: 682 us -> 703 us (1.031)
  local copies, waits for them, and re-layouts: 117 us -> 132 us
  starting transfers between devices: 4.96 us -> 14.8 us
    ppermute x0 -> x3, waiting for transfers between devices: none -> 37.5 us  [the longest x2 37.5 us: ring_gather(): from_left = lax.ppermute(from_left, axis, right)]
    all_gather x1, waiting for transfers between devices: 23.5 us -> 0.01 us  [body(): lax.all_gather(qkv_weight, 'mp', axis=0, tiled=True)]
    all_gather x1, waiting for transfers between devices: 17.5 us -> 2.47 us  [body(): lax.all_gather(down_weight, 'mp', axis=1, tiled=True)]
    ppermute x0 -> x3, starting transfers between devices: none -> 9.59 us  [the longest x2 7.56 us: ring_gather(): from_left = lax.ppermute(from_left, axis, right)]
    dynamic_update_slice x0 -> x4, local copies, waits for them, and re-layouts: none -> 8.57 us  [the longest x2 4.91 us: ring_gather(): lax.dynamic_update_slice_in_dim(filled, from_left, (index - turn) % size...]
    unnamed x106 -> x110, local copies, waits for them, and re-layouts: 22.4 us -> 22.1 us
  transfers between devices with their start and end apart: 9 -> 12, of which waited for: 4 -> 4; matrix products, arithmetic and copies ran while one was open for 38% -> 38% of each run, Pallas kernels for 0% -> 0%
where the time goes in v1:
time: 703 us; the launch traced here: 692 us
  waiting for transfers between devices  225 us (32%)
  matrix products  184 us (26%)
  local copies, waits for them, and re-layouts  132 us (19%)
  other arithmetic  79.1 us (11%)
  blocking collectives  41.2 us (6%)
  between operations  15 us (2%)
  starting transfers between devices  14.8 us (2%)
    unnamed x9, waiting for transfers between devices  106 us
    reduce_scatter x1, waiting for transfers between devices, body(): lax.psum_scatter(slotted.astype(jnp.bfloat16), 'dp', scatter_dimension=0,...  79.2 us
    psum x1, blocking collectives, body(): lax.psum((norm_grad, mask_grad, head_grad, layer_grad, unit_grad), ('dp',...  41.2 us
    dot_general x1, matrix products, body(): jnp.dot(back_rounded, down_full, preferred_element_type=jnp.float32)  38.9 us
    ppermute x2, waiting for transfers between devices, ring_gather(): from_left = lax.ppermute(from_left, axis, right)  37.5 us
    dot_general x4, matrix products, contract_cols(): lax.dot_general(left, right, (((1,), (1,)), ((), ())), preferred_element_...  35.9 us
    unnamed x110, local copies, waits for them, and re-layouts  22.1 us
    dot_general x2, matrix products, contract_rows(): lax.dot_general(left, right, (((0,), (0,)), ((), ())), preferred_element_...  19.1 us
  transfers between devices with their start and end apart: 12, of which 4 were waited for; matrix products, arithmetic and copies ran while one was open for 38% of the time, Pallas kernels for 0%

profile of v1, /device:TPU:0, one launch (start us, length us, event | category | flops | bytes accessed | tf_op | source)
XLA Modules:
  0.0 691.9 jit_solution(1472658092736024290)
XLA Ops:
  12.0 37.5 %collective-permute-done = bf16[768,768]{1,0:T(8,128)(2,1)} collective-permute-done((bf16[768,768]{1,0:T(8,128)(2,1)}, bf16[768,768]{1,0:T(8,128)(2,1)}, u32[]{:S(2)}, u32[]{:S(2)}) %collective-permute-start) | collective-permute-done | bytes 1179680 | tf_op jit(solution)/shard_map/ppermute | solution.py:26
  49.5 7.1 %collective-permute-start.2 = (bf16[768,768]{1,0:T(8,128)(2,1)}, bf16[768,768]{1,0:T(8,128)(2,1)}, u32[]{:S(2)}, u32[]{:S(2)}) collective-permute-start(bf16[768,768]{1,0:T(8,128)(2,1)} %collective-permute-done), channel_id=1, source_target_pairs={{0,1},{1,2},{2,3},{3,0},{4,5},{5,6},{6,7},{7,4},{8,9},{9,10},{10,1... | collective-permute-start | bytes 3538952 | tf_op jit(solution)/shard_map/ppermute | solution.py:26
  56.7 2.6 copy.87
  59.3 2.6 copy.83
  66.3 2.7 broadcast_in_dim.83
  70.2 2.4 constant_dynamic-update-slice_fusion.3
  72.7 2.4 constant_dynamic-update-slice_fusion.2
  75.1 2.5 constant_dynamic-update-slice_fusion.1
  77.6 8.5 %convolution_convert_fusion = bf16[1024,2304]{1,0:T(8,128)(2,1)} fusion(bf16[1024,768]{1,0:T(8,128)(2,1)} %param.23, bf16[768,2304]{1,0:T(8,128)(2,1)} %all-gather.6.cloned.1.call-done), kind=kOutput, calls=%fused_computation.70 | convolution fusion | flops 3626237952 | bytes 9830400 | tf_op jit(solution)/shard_map/dot_general | solution.py:154
  86.1 6.8 copy.84
  92.8 28.7 %while.22 = (s32[]{:T(128)}, f32[2,512,12,64]{1,3,2,0:T(8,128)}, f32[2,12,512]{2,1,0:T(8,128)}, bf16[2,512,2304]{1,2,0:T(8,128)(2,1)}, s32[2,512]{1,0:T(2,128)S(1)}, /*index=5*/s32[]{:T(128)}) while((s32[]{:T(128)}, f32[2,512,12,64]{1,3,2,0:T(8,128)}, f32[2,12,512]{2,1,0:T(8,128)}, bf16[2,512,2304]{1,2,0:T(8,128)(2,1)}, ...), condition=%wide.region_3.4_spmd, body=%wide.region_0.3_spmd.sunk | while | flops 843311104 | bytes 58554572 | solution.py:156
  97.2 3.5 fusion.100
  100.7 5.6 bitcast_dynamic-update-slice_fusion.4
  111.3 3.5 fusion.100
  114.8 5.6 bitcast_dynamic-update-slice_fusion.4
  121.6 4.3 copy.85
  125.9 2.4 copy.125
  129.1 2.8 copy.99
  131.9 3.8 reshape.267
  135.7 6.7 fusion.57
  145.1 11.4 %fusion.54 = f32[1024,3072]{1,0:T(8,128)} fusion(bf16[768,3072]{1,0:T(8,128)(2,1)} %all-gather.10.cloned.1.call-done, f32[1024,768]{0,1:T(8,128)} %copy-done.5, f32[768]{0:T(1024)S(1)} %copy-done.33, f32[768]{0:T(1024)} %param.32, f32[768]{0:T(1024)S(1)} %copy-done.30, f32[1024]{0:T(1024)S(1)} %fusion.52, f32[1024]{0:T(1024)S(1)} %broadcast_multiply_fusion.1), kind=kOutput, calls=%fused_computation.132 | convolution fusion | flops 4836556800 | bytes 20464640 | tf_op jit(solution)/shard_map/dot_general | solution.py:165
  156.5 2.5 all-gather.12.cloned.1.call-done
  158.9 38.9 %multiply_reduce_fusion.1 = (f32[3072]{0:T(1024)}, f32[1024,3072]{1,0:T(8,128)}, f32[1024,3072]{1,0:T(8,128)}) fusion(f32[1024,3072]{1,0:T(8,128)} %fusion.54, bf16[768,3072]{1,0:T(8,128)(2,1)} %all-gather.12.cloned.1.call-done, bf16[1024,768]{0,1:T(8,128)(2,1)} %copy.87, f32[]{:T(128)} %bitcast.21), kind=kOutput, calls=%fused_computation.51 | convolution fusion | flops 5041812480 | bytes 44052484 | tf_op jit(solution)/shard_map/dot_general | solution.py:177
  197.9 16.6 %add_convert_fusion = (bf16[1024,3072]{1,0:T(8,128)(2,1)}, bf16[1024,3072]{1,0:T(8,128)(2,1)}) fusion(f32[1024,3072]{1,0:T(8,128)} %get-tuple-element.182, f32[1024,3072]{1,0:T(8,128)} %get-tuple-element.202, f32[1024,3072]{1,0:T(8,128)S(1)} %bitcast.193, f32[3072]{0:T(1024)S(1)} %copy-done.45), kind=kLoop, calls=%fused_computation.52 | loop fusion | flops 56623104 | bytes 50343936 | tf_op jit(solution)/shard_map/convert_element_type | solution.py:179
  214.6 11.0 %fusion.37 = bf16[3072,1,768]{2,0,1:T(8,128)(2,1)} fusion(bf16[1024,3072]{1,0:T(8,128)(2,1)} %get-tuple-element.192, bf16[1024,768]{0,1:T(8,128)(2,1)S(1)} %copy-done.19, f32[]{:T(128)} %bitcast.21), kind=kOutput, calls=%fused_computation.81 | convolution fusion | flops 4836556800 | bytes 12582916 | tf_op jit(solution)/shard_map/dot_general | solution.py:100
  225.6 8.1 %fusion.36 = bf16[3072,1,768]{2,0,1:T(8,128)(2,1)} fusion(bf16[1024,3072]{1,0:T(8,128)(2,1)S(1)} %copy-done.14, f32[1024,768]{0,1:T(8,128)S(1)} %copy-done.6, f32[768]{0:T(1024)S(1)} %copy-done.34, f32[768]{0:T(1024)S(1)} %copy-done.40, f32[768]{0:T(1024)S(1)} %copy-done.31, f32[1024]{0:T(1024)S(1)} %copy-done.36, f32[1024]{0:T(1024)S(1)} %copy-done.29), kind=kOutput, calls=%fused_computation.80 | convolution fusion | flops 4838916096 | bytes 14173184 | tf_op jit(solution)/shard_map/dot_general | solution.py:100
  233.7 8.2 %pad_maximum_fusion.1 = bf16[3072,2,768]{2,0,1:T(8,128)(2,1)} fusion(bf16[3072,1,768]{2,0,1:T(8,128)(2,1)} %fusion.37, bf16[3072,1,768]{2,0,1:T(8,128)(2,1)} %fusion.36), kind=kLoop, calls=%fused_computation.68 | loop fusion | flops 4718592 | bytes 18874368 | tf_op jit(solution)/shard_map/stack | solution.py:185
  242.1 9.0 %convert_add_fusion = f32[1024,768]{0,1:T(8,128)S(1)} fusion(bf16[1024,768]{0,1:T(8,128)(2,1)} %copy.87, bf16[1024,3072]{1,0:T(8,128)(2,1)} %get-tuple-element.191, bf16[768,3072]{1,0:T(8,128)(2,1)} %all-gather.10.cloned.1.call-done), kind=kOutput, calls=%fused_computation.75 | convolution fusion | flops 4833411072 | bytes 15728640 | tf_op jit(solution)/shard_map/dot_general | solution.py:106
  251.1 14.6 %multiply_reduce_fusion.2 = (f32[768]{0:T(1024)}, f32[1024]{0:T(1024)S(1)}, f32[768]{0:T(1024)}, f32[768]{0:T(1024)}, bf16[1024,768]{0,1:T(8,128)(2,1)}, /*index=5*/f32[]{:T(128)}) fusion(f32[1024,768]{0,1:T(8,128)S(1)} %convert_add_fusion, f32[1024,768]{0,1:T(8,128)S(1)} %copy-done.7, f32[768]{0:T(1024)S(1)} %copy-done.34, f32[1024]{0:T(1024)S(1)} %copy-done.36, ...), kind=kOutput, calls=%fused_computation.87 | convolution fusion | flops 4847563776 | bytes 20477960 | tf_op jit(solution)/shard_map/dot_general | solution.py:106
  266.6 2.6 copy-done.13
  269.2 2.4 multiply_reduce_fusion.3
  272.7 2.6 convolution_convert_fusion.3
  275.3 2.6 copy.88
  277.9 4.2 reshape.245
  282.2 3.1 broadcast_multiply_fusion
  289.4 55.0 %while.23 = (s32[]{:T(128)}, bf16[2,512,2304]{1,2,0:T(8,128)(2,1)}, bf16[2,512,2304]{1,2,0:T(8,128)(2,1)}, s32[2,512]{1,0:T(2,128)S(1)}, f32[2,12,512]{2,1,0:T(8...) while((s32[]{:T(128)}, bf16[2,512,2304]{1,2,0:T(8,128)(2,1)}, bf16[2,512,2304]{1,2,0:T(8,128)(2,1)}, ...), condition=%wide.region_10.11_spmd, body=%wide.region_8.10_spmd.sunk | while | flops 2065033216 | bytes 176027952 | solution.py:200
  293.6 3.1 fusion.106
  296.7 7.1 %multiply_reduce_fusion.10 = (f32[12,512]{1,0:T(8,128)S(1)}, f32[12,512,512]{1,2,0:T(8,128)}) fusion(f32[12,512,512]{1,2,0:T(8,128)S(1)} %fusion.105, f32[12,512]{1,0:T(8,128)S(1)} %dynamic-slice_bitcast_fusion.3, pred[512,512]{0,1:T(8,128)(4,1)S(1)} %broadcast_compare_fusion.5, bf16[512,3,12,64]{0,3,2,1:T(8,128)(2,1)S(1)} %bitcast.186, ...), kind=kOutput, calls=%fused_computation.19.clone.1 | convolution fusion | flops 418375680 | bytes 27058180 | tf_op jit(solution)/shard_map/while/body/eval_jaxpr/qhd,khd->hqk/dot_general | solution.py:82
  303.8 7.2 %multiply_convert_fusion.12 = bf16[12,512,512]{1,2,0:T(8,128)(2,1)S(1)} fusion(f32[12,512,512]{1,2,0:T(8,128)} %get-tuple-element.279, f32[12,512,512]{1,2,0:T(8,128)S(1)} %fusion.105, f32[12,512]{1,0:T(8,128)S(1)} %get-tuple-element.280, f32[12,512]{1,0:T(8,128)S(1)} %dynamic-slice_bitcast_fusion.3, pred[512,512]{0,1:T(8,128)(4,1)S(1)} %broadcast_compare_fusion.5), kind=kLoop, calls=%fused_computation.18.clone.1 | loop fusion | flops 18874368 | bytes 31768576 | tf_op jit(solution)/shard_map/while/body/eval_jaxpr/convert_element_type | solution.py:86
  321.1 3.1 fusion.106
  324.2 7.1 %multiply_reduce_fusion.10 = (f32[12,512]{1,0:T(8,128)S(1)}, f32[12,512,512]{1,2,0:T(8,128)}) fusion(f32[12,512,512]{1,2,0:T(8,128)S(1)} %fusion.105, f32[12,512]{1,0:T(8,128)S(1)} %dynamic-slice_bitcast_fusion.3, pred[512,512]{0,1:T(8,128)(4,1)S(1)} %broadcast_compare_fusion.5, bf16[512,3,12,64]{0,3,2,1:T(8,128)(2,1)S(1)} %bitcast.186, ...), kind=kOutput, calls=%fused_computation.19.clone.1 | convolution fusion | flops 418375680 | bytes 27058180 | tf_op jit(solution)/shard_map/while/body/eval_jaxpr/qhd,khd->hqk/dot_general | solution.py:82
  331.3 7.1 %multiply_convert_fusion.12 = bf16[12,512,512]{1,2,0:T(8,128)(2,1)S(1)} fusion(f32[12,512,512]{1,2,0:T(8,128)} %get-tuple-element.279, f32[12,512,512]{1,2,0:T(8,128)S(1)} %fusion.105, f32[12,512]{1,0:T(8,128)S(1)} %get-tuple-element.280, f32[12,512]{1,0:T(8,128)S(1)} %dynamic-slice_bitcast_fusion.3, pred[512,512]{0,1:T(8,128)(4,1)S(1)} %broadcast_compare_fusion.5), kind=kLoop, calls=%fused_computation.18.clone.1 | loop fusion | flops 18874368 | bytes 31768576 | tf_op jit(solution)/shard_map/while/body/eval_jaxpr/convert_element_type | solution.py:86
  344.3 10.1 %copy.95 = bf16[2,512,2304]{1,0,2:T(2,128)(2,1)} copy(bf16[2,512,2304]{1,2,0:T(8,128)(2,1)} %get-tuple-element.76) | data formatting | bytes 9437184 | tf_op jit(solution)/shard_map/while | solution.py:200
  354.4 8.7 %reshape_reshape.3 = bf16[1024,6,384]{0,2,1:T(8,128)(2,1)} reshape(bf16[2,512,2304]{1,0,2:T(2,128)(2,1)} %copy.95) | data formatting | bytes 9437184 | tf_op jit(solution)/shard_map/reshape;reshape | solution.py:215
  363.1 6.6 convert_bitcast_fusion
  371.0 2.7 pad_maximum_fusion.2
  373.8 4.3 copy.102
  378.1 4.0 copy.103
  382.1 4.6 all-to-all-start
  389.4 103.4 %all-reduce.4.cloned.1.call-done = bf16[16,4,96,384]{3,2,1,0:T(8,128)(2,1)} async-done(((bf16[16,4,96,384]{3,2,1,0:T(8,128)(2,1)}), bf16[16,4,96,384]{3,2,1,0:T(8,128)(2,1)}) %all-reduce.4.cloned.1.call-update) | async-done | bytes 4718608
  492.9 3.1 dynamic-slice_bitcast_fusion.1
  495.9 4.9 copy.104
  500.9 5.1 convert_element_type.132
  510.4 5.0 gather_fusion
  515.3 4.8 select_convert_fusion
  520.5 79.2 %reduce-scatter.8.cloned.1.call-done = bf16[6,96,384]{2,1,0:T(8,128)(2,1)} async-done(((bf16[48,96,384]{2,1,0:T(8,128)(2,1)}), bf16[6,96,384]{2,1,0:T(8,128)(2,1)}) %reduce-scatter.8.cloned.1.call-update) | async-done | bytes 442384 | tf_op jit(solution)/shard_map/reduce_scatter | solution.py:248
  603.0 5.5 multiply_reduce_fusion.5
  608.6 41.2 %all-reduce.1 = (f32[12]{0:T(128)}, f32[3072]{0:T(1024)}, f32[768]{0:T(1024)}, f32[2]{0:T(128)}, f32[2,768]{1,0:T(2,128)}) all-reduce(f32[12]{0:T(128)} %multiply_reduce_fusion.5, f32[3072]{0:T(1024)} %get-tuple-element.181, f32[768]{0:T(1024)} %get-tuple-element.152, ...), channel_id=1, replica_groups=mesh['dp'=8,'mp'=4] {'dp','mp'}, use_global_device_ids=true, to_apply=%region_12.13 | all-reduce | flops 5390 | bytes 43120 | tf_op jit(solution)/shard_map/psum | solution.py:266
  649.7 6.7 copy.91
  656.5 2.6 copy.107
  659.0 9.8 %add_add_fusion.1 = f32[1024,768]{0,1:T(8,128)} fusion(f32[1024,768]{0,1:T(8,128)} %copy-done.12, bf16[1024,2304]{1,0:T(8,128)(2,1)} %bitcast.204, bf16[768,2304]{1,0:T(8,128)(2,1)} %all-gather.6.cloned.1.call-done, f32[1024]{0:T(1024)S(1)} %copy-done.49), kind=kOutput, calls=%fused_computation.99 | convolution fusion | flops 3625451520 | bytes 14553088 | tf_op jit(solution)/shard_map/dot_general | solution.py:106
  668.8 3.6 copy.108
  675.0 2.9 fusion.61
  677.9 3.6 fusion.60
  (243 shorter events, 67.7 us)
Async XLA Ops:
  7.2 670.7 %copy-start = (f32[6,384,384]{2,1,0:T(8,128)S(1)}, f32[6,384,384]{2,1,0:T(8,128)}, u32[]{:S(2)}) copy-start(f32[6,384,384]{2,1,0:T(8,128)} %param.41) | copy-start | bytes 10616836
  7.2 70.4 %all-gather.6.cloned.1.call-start = ((), (), s32[]{:S(2)}) async-start(), calls=%async_computation.3 | async-start | bytes 4423680 | tf_op jit(solution)/shard_map/all_gather | solution.py:149
  7.9 127.8 %all-gather.8.cloned.1.call-start = ((), (), s32[]{:S(2)}) async-start(), calls=%async_computation.4 | async-start | bytes 1474560 | tf_op jit(solution)/shard_map/all_gather | solution.py:150
  8.7 136.4 %all-gather.10.cloned.1.call-start = ((), (), s32[]{:S(2)}) async-start(), calls=%async_computation.5 | async-start | bytes 5898240 | tf_op jit(solution)/shard_map/all_gather | solution.py:151
  9.4 52.4 %copy-start.55 = (s32[12]{0:T(128)S(1)}, s32[12]{0:T(128)}, u32[]{:S(2)}) copy-start(s32[12]{0:T(128)} %param.25) | copy-start | bytes 148
  9.4 53.6 %copy-start.51 = (s32[768]{0:T(1024)S(1)}, s32[768]{0:T(1024)}, u32[]{:S(2)}) copy-start(s32[768]{0:T(1024)} %param.27) | copy-start | bytes 9220
  9.4 149.5 %all-gather.12.cloned.1.call-start = ((), (), s32[]{:S(2)}) async-start(), calls=%async_computation.6 | async-start | bytes 5898240 | tf_op jit(solution)/shard_map/all_gather | solution.py:175
  9.5 40.0 %collective-permute-start = (bf16[768,768]{1,0:T(8,128)(2,1)}, bf16[768,768]{1,0:T(8,128)(2,1)}, u32[]{:S(2)}, u32[]{:S(2)}) collective-permute-start(bf16[768,768]{1,0:T(8,128)(2,1)} %param.34), channel_id=1, source_target_pairs={{0,1},{1,2},{2,3},{3,0},{4,5},{5,6},{6,7},{7,4},{8,9},{9,10},{10,1... | collective-permute-start | bytes 3538952 | tf_op jit(solution)/shard_map/ppermute | solution.py:26
  10.0 62.7 %collective-permute-start.1 = (bf16[768,768]{1,0:T(8,128)(2,1)}, bf16[768,768]{1,0:T(8,128)(2,1)}, u32[]{:S(2)}, u32[]{:S(2)}) collective-permute-start(bf16[768,768]{1,0:T(8,128)(2,1)} %param.34), channel_id=1, source_target_pairs={{0,3},{1,0},{2,1},{3,2},{4,7},{5,4},{6,5},{7,6},{8,11},{9,8},{10,9... | collective-permute-start | bytes 3538952 | tf_op jit(solution)/shard_map/ppermute | solution.py:31
  49.5 25.7 %collective-permute-start.2 = (bf16[768,768]{1,0:T(8,128)(2,1)}, bf16[768,768]{1,0:T(8,128)(2,1)}, u32[]{:S(2)}, u32[]{:S(2)}) collective-permute-start(bf16[768,768]{1,0:T(8,128)(2,1)} %collective-permute-done), channel_id=1, source_target_pairs={{0,1},{1,2},{2,3},{3,0},{4,5},{5,6},{6,7},{7,4},{8,9},{9,10},{10,1... | collective-permute-start | bytes 3538952 | tf_op jit(solution)/shard_map/ppermute | solution.py:26
  56.5 317.2 %reduce-scatter.6.cloned.1.call-start = ((), (), s32[]{:S(2)}) async-start(), calls=%async_computation.7 | async-start | bytes 11796480 | tf_op jit(solution)/shard_map/reduce_scatter | solution.py:184
  64.9 4.1 copy-start.17
  86.1 6.8 copy-start.43
  93.1 4.1 copy-start.4
  100.7 5.6 copy-start.37
  107.2 4.1 copy-start.4
  114.8 5.6 copy-start.37
  135.7 9.4 %copy-start.30 = (f32[768]{0:T(1024)S(1)}, f32[768]{0:T(1024)}, u32[]{:S(2)}) copy-start(f32[768]{0:T(1024)} %param.31) | copy-start | bytes 9220
  135.7 9.4 %copy-start.33 = (f32[768]{0:T(1024)S(1)}, f32[768]{0:T(1024)}, u32[]{:S(2)}) copy-start(f32[768]{0:T(1024)} %convert_element_type.114) | copy-start | bytes 9220
  142.4 14.0 %copy-start.28 = (f32[1024]{0:T(1024)}, f32[1024]{0:T(1024)S(1)}, u32[]{:S(2)}) copy-start(f32[1024]{0:T(1024)S(1)} %broadcast_multiply_fusion.1) | copy-start | bytes 12292
  145.1 11.4 %copy-start.35 = (f32[1024]{0:T(1024)}, f32[1024]{0:T(1024)S(1)}, u32[]{:S(2)}) copy-start(f32[1024]{0:T(1024)S(1)} %fusion.52) | copy-start | bytes 12292
  158.9 38.9 %slice-start = ((s8[12582912]{0:T(1024)(128)(4,1)}), s8[4194304]{0:T(1024)(128)(4,1)S(1)}, s32[]{:S(2)}) async-start(s8[12582912]{0:T(1024)(128)(4,1)} %bitcast.192), calls=%async_computation.11 | async-start | bytes 8388608
  158.9 38.9 %slice-start.1 = ((s8[12582912]{0:T(1024)(128)(4,1)}), s8[4194304]{0:T(1024)(128)(4,1)S(1)}, s32[]{:S(2)}) async-start(s8[12582912]{0:T(1024)(128)(4,1)} %bitcast.192), calls=%async_computation.12 | async-start | bytes 8388608
  158.9 38.9 %slice-start.2 = ((s8[12582912]{0:T(1024)(128)(4,1)}), s8[4194304]{0:T(1024)(128)(4,1)S(1)}, s32[]{:S(2)}) async-start(s8[12582912]{0:T(1024)(128)(4,1)} %bitcast.192), calls=%async_computation.13 | async-start | bytes 8388608
  158.9 38.9 %copy-start.45 = (f32[3072]{0:T(1024)S(1)}, f32[3072]{0:T(1024)}, u32[]{:S(2)}) copy-start(f32[3072]{0:T(1024)} %convert_element_type.116) | copy-start | bytes 36868
  197.9 16.6 %copy-start.19 = (bf16[1024,768]{0,1:T(8,128)(2,1)S(1)}, bf16[1024,768]{0,1:T(8,128)(2,1)}, u32[]{:S(2)}) copy-start(bf16[1024,768]{0,1:T(8,128)(2,1)} %copy.87) | copy-start | bytes 4718596
  214.5 11.1 %copy-start.6 = (f32[1024,768]{0,1:T(8,128)S(1)}, f32[1024,768]{0,1:T(8,128)}, u32[]{:S(2)}) copy-start(f32[1024,768]{0,1:T(8,128)} %copy-done.5) | copy-start | bytes 9437188
  214.5 11.1 %copy-start.14 = (bf16[1024,3072]{1,0:T(8,128)(2,1)S(1)}, bf16[1024,3072]{1,0:T(8,128)(2,1)}, u32[]{:S(2)}) copy-start(bf16[1024,3072]{1,0:T(8,128)(2,1)} %get-tuple-element.191) | copy-start | bytes 18874372
  214.5 11.1 %copy-start.29 = (f32[1024]{0:T(1024)S(1)}, f32[1024]{0:T(1024)}, u32[]{:S(2)}) copy-start(f32[1024]{0:T(1024)} %copy-done.28) | copy-start | bytes 12292
  214.5 11.0 %copy-start.31 = (f32[768]{0:T(1024)S(1)}, f32[768]{0:T(1024)}, u32[]{:S(2)}) copy-start(f32[768]{0:T(1024)} %param.31) | copy-start | bytes 9220
  214.5 11.0 %copy-start.34 = (f32[768]{0:T(1024)S(1)}, f32[768]{0:T(1024)}, u32[]{:S(2)}) copy-start(f32[768]{0:T(1024)} %convert_element_type.114) | copy-start | bytes 9220
  214.6 11.0 %copy-start.36 = (f32[1024]{0:T(1024)S(1)}, f32[1024]{0:T(1024)}, u32[]{:S(2)}) copy-start(f32[1024]{0:T(1024)} %copy-done.35) | copy-start | bytes 12292
  214.6 11.0 %copy-start.40 = (f32[768]{0:T(1024)S(1)}, f32[768]{0:T(1024)}, u32[]{:S(2)}) copy-start(f32[768]{0:T(1024)} %param.32) | copy-start | bytes 9220
  242.0 250.9 %all-reduce.4.cloned.1.call-start = ((), (), s32[]{:S(2)}) async-start(), calls=%async_computation.10 | async-start | bytes 9437184
  242.0 9.0 %copy-start.7 = (f32[1024,768]{0,1:T(8,128)S(1)}, f32[1024,768]{0,1:T(8,128)}, u32[]{:S(2)}) copy-start(f32[1024,768]{0,1:T(8,128)} %copy-done.5) | copy-start | bytes 9437188
  242.0 9.0 %copy-start.20 = (bf16[1024,768]{0,1:T(8,128)(2,1)S(1)}, bf16[1024,768]{0,1:T(8,128)(2,1)}, u32[]{:S(2)}) copy-start(bf16[1024,768]{0,1:T(8,128)(2,1)} %copy.87) | copy-start | bytes 4718596
  242.0 9.0 %copy-start.41 = (f32[768]{0:T(1024)S(1)}, f32[768]{0:T(1024)}, u32[]{:S(2)}) copy-start(f32[768]{0:T(1024)} %param.32) | copy-start | bytes 9220
  251.1 14.6 %copy-start.47 = (f32[1024]{0:T(1024)S(1)}, f32[1024]{0:T(1024)}, u32[]{:S(2)}) copy-start(f32[1024]{0:T(1024)} %copy-done.46) | copy-start | bytes 12292
  265.7 3.5 copy-start.13
  266.6 5.0 copy-start.12
  266.6 5.0 copy-start.48
  269.2 3.5 copy-start.24
  275.3 6.9 copy-start.54
  282.2 4.6 copy-start.21
  282.2 4.6 copy-start.23
  291.2 5.4 copy-start.1
  303.8 7.2 %copy-start.2 = (bf16[1,512,2304]{1,2,0:T(8,128)(2,1)S(1)}, bf16[1,512,2304]{1,2,0:T(8,128)(2,1)}, u32[]{:S(2)}) copy-start(bf16[1,512,2304]{1,2,0:T(8,128)(2,1)} %copy-done.1) | copy-start | bytes 7077892 | tf_op jit(solution)/shard_map/while
  311.0 3.4 slice-start.3
  318.7 5.5 copy-start.1
  331.3 7.1 %copy-start.2 = (bf16[1,512,2304]{1,2,0:T(8,128)(2,1)S(1)}, bf16[1,512,2304]{1,2,0:T(8,128)(2,1)}, u32[]{:S(2)}) copy-start(bf16[1,512,2304]{1,2,0:T(8,128)(2,1)} %copy-done.1) | copy-start | bytes 7077892 | tf_op jit(solution)/shard_map/while
  338.5 3.4 slice-start.3
  382.1 4.7 copy-start.57
  382.1 5.3 copy-start.56
  382.1 113.9 %all-to-all-start = ((bf16[2,2,4,96,768]{4,3,1,0,2:T(8,128)(2,1)}), bf16[2,2,4,96,768]{4,3,1,0,2:T(8,128)(2,1)}, u32[]{:S(2)}, u32[]{:S(2)}) async-start(bf16[2,2,4,96,768]{4,3,1,0,2:T(8,128)(2,1)} %copy.103), calls=%async_computation.1 | async-start | bytes 4718592 | tf_op jit(solution)/shard_map/all_to_all | solution.py:237
  386.7 213.0 %reduce-scatter.8.cloned.1.call-start = ((), (), s32[]{:S(2)}) async-start(), calls=%async_computation.8 | async-start | bytes 3981312 | tf_op jit(solution)/shard_map/reduce_scatter | solution.py:248
  520.2 79.5 %copy-start.42 = (f32[768]{0:T(1024)S(1)}, f32[768]{0:T(1024)}, u32[]{:S(2)}) copy-start(f32[768]{0:T(1024)} %param.32) | copy-start | bytes 9220
  520.2 79.6 %copy-start.32 = (f32[768]{0:T(1024)S(1)}, f32[768]{0:T(1024)}, u32[]{:S(2)}) copy-start(f32[768]{0:T(1024)} %param.31) | copy-start | bytes 9220
  520.2 154.8 %all-gather.14.cloned.1.call-start = ((), (), s32[]{:S(2)}) async-start(), calls=%async_computation.9 | async-start | bytes 2211840 | tf_op jit(solution)/shard_map/all_gather | solution.py:251
  649.7 9.3 %copy-start.49 = (f32[1024]{0:T(1024)S(1)}, f32[1024]{0:T(1024)}, u32[]{:S(2)}) copy-start(f32[1024]{0:T(1024)} %copy-done.48) | copy-start | bytes 12292
  668.8 3.6 copy-start.50
  675.0 2.9 copy-start.25
  677.9 3.6 copy-start.11
  677.9 3.6 copy-start.18
  677.9 3.6 copy-start.26
  (22 other events, 37.9 us)
Sparse Core Ops, SparseCore 0:
  9.6 51.3 all-gather.5
  62.5 17.7 all-gather.7
  81.9 38.0 all-gather.9
  121.4 37.4 all-gather.11
  242.1 78.4 reduce-scatter.5
  373.9 118.9 all-reduce.3
  520.3 79.3 reduce-scatter.7
  601.3 20.8 all-gather.13
